TPU v7x, 32 devices: a whole 2x2x4 slice. The times are simulated.
32 devices in a mesh: gx: 8 (over z, y), gy: 4 (over x, core).
Axes of the slice: x: 2, y: 2, z: 4, core: 2. Of those that a mesh axis runs over, the one named last changes fastest.
Arguments:
- features: bfloat16 [1024, 256, 128], P('gx', 'gy'), may hold values from -6 to 6
- cotangent: bfloat16 [1024, 256, 128], P('gx', 'gy'), may hold values from -31 to 31
- kernel: float32 [7, 7, 128], replicated, may hold values from -0.875 to 0.875
- kernel_bias: float32 [128], replicated, may hold values from -3 to 3
- norm_gain: float32 [128], replicated, may hold values from 0.1 to 1.9
- norm_shift: float32 [128], replicated, may hold values from -3 to 3
- w_up: bfloat16 [128, 512], replicated, may hold values from -0.5 to 0.5
- b_up: float32 [512], replicated, may hold values from -3 to 3
- w_down: bfloat16 [512, 128], replicated, may hold values from -0.25 to 0.25
- b_down: float32 [128], replicated, may hold values from -3 to 3
- layer_scale: float32 [128], replicated, may hold values from 0.3 to 3
Outputs:
- d_features: bfloat16 [1024, 256, 128], P('gx', 'gy')
- d_kernel: float32 [7, 7, 128], replicated
- d_kernel_bias: float32 [128], replicated
- d_norm_gain: float32 [128], replicated
- d_norm_shift: float32 [128], replicated
- d_w_up: float32 [128, 512], replicated
- d_b_up: float32 [512], replicated
- d_w_down: float32 [512, 128], replicated
- d_b_down: float32 [128], replicated
- d_layer_scale: float32 [128], replicated
All inputs are finite; a program needn't handle non-finite values.
Results may differ from a plain program's by a relative error of at most 0.0072.
Values may be sent and summed in bfloat16 or wider, within the bound.
A program may use at most 64 MiB of HBM per device.

v0:
```python
import functools
import math

import jax
import jax.numpy as jnp
from jax import lax
from jax.experimental import pallas as pl
from jax.experimental.pallas import tpu as pltpu
from jax.sharding import PartitionSpec as P

EPSILON = 1e-06
F32 = jnp.float32
BF16 = jnp.bfloat16
VMEM_BYTES = 60 * 1024 * 1024


def dot(left, right):
    return jnp.dot(left, right, preferred_element_type=F32)


def extended(cells, sides, width):
    for axis, dim in sides:
        count = lax.axis_size(axis)
        head = lax.slice_in_dim(cells, 0, width, axis=dim)
        tail = lax.slice_in_dim(cells, cells.shape[dim] - width, cells.shape[dim], axis=dim)
        cells = jnp.concatenate(
            [
                lax.ppermute(tail, axis, [(i, (i + 1) % count) for i in range(count)]),
                cells,
                lax.ppermute(head, axis, [((i + 1) % count, i) for i in range(count)]),
            ],
            axis=dim,
        )
    return cells


def mask_edges(padded, width):
    col_total = padded.shape[1]
    inner_cols = col_total - 2 * width
    grid_cols = inner_cols * lax.axis_size("gy")
    col_place = lax.axis_index("gy") * inner_cols + lax.iota(jnp.int32, col_total) - width
    keep_mask = (col_place >= 0) & (col_place < grid_cols)
    return jnp.where(keep_mask[None, :, None], padded, jnp.zeros((), padded.dtype))


def widened(cells, reach):
    padded = mask_edges(extended(cells, (("gx", 0), ("gy", 1)), reach), reach)
    extra = -padded.shape[1] % 16
    return jnp.pad(padded, ((0, 0), (0, extra), (0, 0)))


def tap_weights(kernel):
    taps, _, chans = kernel.shape
    pairs = (taps + 1) // 2
    framed = jnp.pad(kernel, ((1, 1), (0, 0), (0, 0)))
    eye = jnp.eye(chans, dtype=F32)
    blocks = []
    for q in range(pairs):
        top = jnp.concatenate([framed[2 * q + 1, :, :, None] * eye, framed[2 * q, :, :, None] * eye], 2)
        low = jnp.concatenate([framed[2 * q + 2, :, :, None] * eye, framed[2 * q + 1, :, :, None] * eye], 2)
        blocks.append(jnp.concatenate([top, low], 1).reshape(taps * 2 * chans, 2 * chans))
    return jnp.stack(blocks).astype(BF16)


def spread_taps(padded, wide, shifted, taps):
    pairs, cols, _ = shifted.shape
    chans = padded.shape[2]

    def one(j, carry):
        for s in range(2):
            wide[s] = padded[2 * j + s].astype(F32)
            for b in range(taps):
                at = (2 * b + s) * chans
                shifted[j, :, at : at + chans] = wide[s, b : b + cols, :].astype(BF16)
        return carry

    lax.fori_loop(0, pairs, one, 0)


def conv_pairs(shifted, weights, first, count):
    pairs, cols, depth = shifted.shape
    total = None
    for q in range(weights.shape[0]):
        rows = shifted[pl.ds(first + q, count)].reshape(count * cols, depth)
        part = dot(rows, weights[q])
        total = part if total is None else total + part
    return total


def forward_back(
    taps,
    count,
    padded,
    cot,
    conv_w,
    kbias,
    gain,
    shift,
    w_up,
    w_up_t,
    b_up,
    w_dn_t,
    d_conv,
    g_up,
    g_dn,
    g_bup,
    g_small,
    g_kern,
    wide,
    shifted,
    d_turned,
):
    rows, cols, chans = cot.shape
    half = count * cols
    spread_taps(padded, wide, shifted, taps)
    g_up[...] = jnp.zeros_like(g_up)
    g_dn[...] = jnp.zeros_like(g_dn)
    g_bup[...] = jnp.zeros_like(g_bup)
    g_small[...] = jnp.zeros_like(g_small)

    def chunk(i, carry):
        first = i * count
        pair_out = conv_pairs(shifted, conv_w, first, count)
        conv = jnp.concatenate([pair_out[:, :chans], pair_out[:, chans:]], 0) + kbias[...]
        cot_rows = [cot[2 * (first + k) + p] for p in range(2) for k in range(count)]
        cotan = jnp.concatenate(cot_rows, 0)
        centred = conv - jnp.mean(conv, axis=-1, keepdims=True)
        inv_std = lax.rsqrt(jnp.mean(centred * centred, axis=-1, keepdims=True) + EPSILON)
        normed = centred * inv_std
        normal_out = (normed * gain[...] + shift[...]).astype(BF16)
        hidden = dot(normal_out, w_up[...]) + b_up[...]
        bell = jnp.exp(hidden * hidden * -0.5)
        place = 1.0 / (1.0 + jnp.abs(hidden) * (0.3275911 * 0.7071067811865476))
        tail = place * (
            0.127414796
            + place * (-0.142248368 + place * (0.7107068705 + place * (-0.7265760135 + place * 0.5307027145)))
        )
        tail = tail * bell
        phi = jnp.where(hidden >= 0.0, 1.0 - tail, tail)
        active = (hidden * phi).astype(BF16)
        slope = phi + hidden * bell * 0.3989422804014327
        d_active = dot(cotan, w_dn_t[...])
        d_hidden_f = d_active * slope
        d_hidden = d_hidden_f.astype(BF16)
        d_normal = dot(d_hidden, w_up_t[...])
        g = d_normal * gain[...]
        gn = g * normed
        d_cv = inv_std * (
            g - jnp.mean(g, axis=-1, keepdims=True) - normed * jnp.mean(gn, axis=-1, keepdims=True)
        )
        cot_f = cotan.astype(F32)
        g_up[...] += dot(normal_out.T, d_hidden)
        g_dn[...] += dot(cotan.T, active)
        g_bup[...] += jnp.sum(d_hidden_f, axis=0, keepdims=True)
        g_small[0:1] += jnp.sum(d_cv, axis=0, keepdims=True)
        g_small[1:2] += jnp.sum(d_normal * normed, axis=0, keepdims=True)
        g_small[2:3] += jnp.sum(d_normal, axis=0, keepdims=True)
        g_small[3:4] += jnp.sum(cot_f, axis=0, keepdims=True)
        d_low = d_cv.astype(BF16)
        for p in range(2):
            part = d_low[p * half : (p + 1) * half]
            d_turned[p * chans : (p + 1) * chans, pl.ds(pl.multiple_of(first * cols, half), half)] = part.T
            for k in range(count):
                d_conv[2 * (first + k) + p] = part[k * cols : (k + 1) * cols]
        return carry

    lax.fori_loop(0, rows // (2 * count), chunk, 0)

    eye = (
        lax.broadcasted_iota(jnp.int32, (chans, chans), 0)
        == lax.broadcasted_iota(jnp.int32, (chans, chans), 1)
    ).astype(F32)
    pairs = rows // 2

    def tap(b, carry):
        lines = [None] * (taps + 1)
        for q in range(conv_w.shape[0]):
            lanes = pl.ds(pl.multiple_of(b * (2 * chans), 2 * chans), 2 * chans)
            cells = shifted[q : q + pairs, :, lanes].reshape(pairs * cols, 2 * chans)
            both = dot(d_turned[...], cells)
            for p in range(2):
                for s in range(2):
                    a = 2 * q + s - p
                    if 0 <= a < taps:
                        block = both[p * chans : (p + 1) * chans, s * chans : (s + 1) * chans]
                        line = jnp.sum(block * eye, axis=0, keepdims=True)
                        lines[a] = line if lines[a] is None else lines[a] + line
        lines[taps] = jnp.zeros((1, chans), F32)
        g_kern[b] = jnp.concatenate(lines, 0)
        return carry

    lax.fori_loop(0, taps, tap, 0)


def spread_kernel(taps, count, padded, cot, conv_w, out, wide, shifted):
    rows, cols, chans = cot.shape
    spread_taps(padded, wide, shifted, taps)

    def chunk(i, carry):
        first = i * count
        pair_out = conv_pairs(shifted, conv_w, first, count)
        for p in range(2):
            for k in range(count):
                row = 2 * (first + k) + p
                part = pair_out[k * cols : (k + 1) * cols, p * chans : (p + 1) * chans]
                out[row] = (cot[row].astype(F32) + part).astype(BF16)
        return carry

    lax.fori_loop(0, rows // (2 * count), chunk, 0)


def local(
    features,
    cotangent,
    kernel,
    kernel_bias,
    norm_gain,
    norm_shift,
    w_up,
    b_up,
    w_down,
    b_down,
    layer_scale,
):
    taps = kernel.shape[0]
    reach = taps // 2
    rows, cols, chans = features.shape
    units = w_up.shape[1]
    padded_x = widened(features, reach)
    pairs = padded_x.shape[0] // 2
    shapes = jax.ShapeDtypeStruct
    scratch = [
        pltpu.VMEM((2, padded_x.shape[1], chans), F32),
        pltpu.VMEM((pairs, cols, taps * 2 * chans), BF16),
    ]
    vmem = pl.BlockSpec(memory_space=pltpu.VMEM)
    params = pltpu.CompilerParams(vmem_limit_bytes=VMEM_BYTES)
    count = 4
    scaled_down = (w_down.T.astype(F32) * layer_scale[:, None]).astype(BF16)
    with jax.named_scope("forward_back"):
        d_conv, g_up, g_dn, g_bup, g_small, g_kern = pl.pallas_call(
            functools.partial(forward_back, taps, count),
            out_shape=[
                shapes((rows, cols, chans), BF16),
                shapes((chans, units), F32),
                shapes((chans, units), F32),
                shapes((1, units), F32),
                shapes((8, chans), F32),
                shapes((taps, taps + 1, chans), F32),
            ],
            in_specs=[vmem] * 10,
            out_specs=[vmem] * 6,
            scratch_shapes=scratch + [pltpu.VMEM((2 * chans, rows * cols // 2), BF16)],
            compiler_params=params,
        )(
            padded_x,
            cotangent,
            tap_weights(kernel),
            kernel_bias[None],
            norm_gain[None],
            norm_shift[None],
            w_up,
            w_up.T,
            b_up[None],
            scaled_down,
        )
    padded_d = widened(d_conv, reach)
    sums = lax.psum((g_up, g_dn, g_bup, g_small, g_kern), ("gx", "gy"))
    with jax.named_scope("spread"):
        d_features = pl.pallas_call(
            functools.partial(spread_kernel, taps, count),
            out_shape=shapes((rows, cols, chans), BF16),
            in_specs=[vmem] * 3,
            out_specs=vmem,
            scratch_shapes=scratch,
            compiler_params=params,
        )(padded_d, cotangent, tap_weights(kernel[::-1, ::-1]))
    factor = 1.0 / math.sqrt(rows * cols * lax.axis_size("gx") * lax.axis_size("gy"))
    g_up, g_dn, g_bup, g_small, g_kern = [entry * factor for entry in sums]
    d_wdown = g_dn.T * layer_scale
    cot_sum = g_small[3]
    d_lscale = jnp.sum(g_dn.T * w_down.astype(F32), axis=0) + b_down * cot_sum
    return (
        d_features,
        jnp.swapaxes(g_kern[:, :taps], 0, 1),
        g_small[0],
        g_small[1],
        g_small[2],
        g_up,
        g_bup[0],
        d_wdown,
        layer_scale * cot_sum,
        d_lscale,
    )


def solution(mesh):
    placed = (P("gx", "gy", None), P("gx", "gy", None), P(), P(), P(), P(), P(), P(), P(), P(), P())
    return jax.shard_map(
        local,
        mesh=mesh,
        in_specs=placed,
        out_specs=(P("gx", "gy", None), P(), P(), P(), P(), P(), P(), P(), P(), P()),
        check_vma=False,
    )
```

profile of v0, /device:TPU:0, one launch (start us, length us, event | category | flops | bytes accessed | tf_op | source)
XLA Modules:
  0.0 309.0 jit_solution(16395151181036343290)
XLA Ops:
  7.2 0.8 fusion.17
  8.1 3.0 collective-permute-start
  11.1 3.1 %collective-permute-start.1 = (bf16[3,64,128]{2,1,0:T(8,128)(2,1)S(1)}, bf16[3,64,128]{2,1,0:T(8,128)(2,1)S(1)}, u32[]{:S(2)}, u32[]{:S(2)}) collective-permute-start(bf16[3,64,128]{2,1,0:T(8,128)(2,1)S(1)} %get-tuple-element.43), channel_id=1, source_target_pairs={{4,0},{8,4},{12,8},{16,12},{20,16},{24,20},{28,24},{0,28},{5,1},{9... | collective-permute-start | bytes 147464 | tf_op jit(solution)/shard_map/ppermute | solution.py:30
  14.2 0.8 fusion.18
  15.1 1.0 copy.22
  16.1 2.0 multiply_convert_fusion.6
  18.1 3.2 %fusion.4 = (bf16[7,256,256]{2,1,0:T(8,128)(2,1)S(1)}, bf16[7,256,256]{2,1,0:T(8,128)(2,1)S(1)}, bf16[7,256,256]{2,1,0:T(8,128)(2,1)S(1)}, bf16[7,256,256]{2,1,0:T(8,128)(2,1)S(1)}) fusion(bf16[7,128,128]{2,1,0:T(8,128)(2,1)S(1)} %get-tuple-element.68, bf16[7,128,128]{2,1,0:T(8,128)(2,1)S(1)} %get-tuple-element.56, ...), kind=kLoop, calls=%fused_computation.10 | loop fusion | flops 14680064 | bytes 5275648 | tf_op jit(solution)/shard_map/forward_back/concatenate | solution.py:61
  21.3 2.1 pad_maximum_fusion.conv_w
  23.4 3.1 %fusion.5 = (bf16[7,256,256]{2,1,0:T(8,128)(2,1)S(1)}, bf16[7,256,256]{2,1,0:T(8,128)(2,1)S(1)}, bf16[7,256,256]{2,1,0:T(8,128)(2,1)S(1)}, bf16[7,256,256]{2,1,0:T(8,128)(2,1)S(1)}) fusion(bf16[7,128,128]{2,1,0:T(8,128)(2,1)S(1)} %get-tuple-element.55, bf16[7,128,128]{2,1,0:T(8,128)(2,1)S(1)} %get-tuple-element.62, ...), kind=kLoop, calls=%fused_computation.11 | loop fusion | flops 14680064 | bytes 5275648 | tf_op jit(solution)/shard_map/spread/concatenate | solution.py:61
  26.5 2.0 pad_maximum_fusion.1.conv_w
  29.3 0.7 copy.21
  30.6 1.7 collective-permute-start.3
  32.3 2.7 collective-permute-done.2
  35.6 1.7 maximum_select_fusion
  37.3 2.1 pad.18.padded
  39.4 78.0 %forward_back.1 = (bf16[128,64,128]{2,1,0:T(8,128)(2,1)}, f32[128,512]{1,0:T(8,128)}, f32[128,512]{1,0:T(8,128)}, f32[1,512]{1,0:T(1,128)}, f32[8,128]{1,0:T(8,128)}, /*index=5*/f32[7,8,128]{2,1,0:T(8,128)}) custom-call(bf16[134,80,128]{2,1,0:T(8,128)(2,1)} %pad.18.padded, bf16[128,64,128]{2,1,0:T(8,128)(2,1)} %cot.3, ...), custom_call_target="tpu_custom_call" | custom-call | tf_op jit(solution)/shard_map/forward_back/pallas_call | solution.py:241
  117.4 38.9 %all-reduce.6 = (f32[7,8,128]{2,1,0:T(8,128)S(1)}, f32[8,128]{1,0:T(8,128)S(1)}, f32[1,512]{1,0:T(1,128)S(1)}) all-reduce(f32[7,8,128]{2,1,0:T(8,128)} %get-tuple-element.17, f32[8,128]{1,0:T(8,128)} %get-tuple-element.18, f32[1,512]{1,0:T(1,128)} %get-tuple-element.20), channel_id=1, replica_groups=mesh['gx'=8,'gy'=4] {'gx','gy'}, use_global_device_ids=true, to_apply=%region_0.1 | all-reduce | flops 8704 | bytes 69632 | tf_op jit(solution)/shard_map/psum | solution.py:268
  156.4 0.8 fusion.16
  157.2 2.3 collective-permute-start.4
  160.0 2.5 collective-permute-start.5
  162.5 1.6 collective-permute-done.4
  164.1 1.9 constant_dynamic-update-slice_fusion.4
  166.2 1.7 collective-permute-start.7
  169.1 1.5 collective-permute-done.6
  170.6 1.1 collective-permute-done.7
  171.7 1.7 maximum_select_fusion.1
  173.4 2.0 pad.19.padded
  175.4 25.2 %spread.1 = bf16[128,64,128]{2,1,0:T(8,128)(2,1)} custom-call(bf16[134,80,128]{2,1,0:T(8,128)(2,1)} %pad.19.padded, bf16[128,64,128]{2,1,0:T(8,128)(2,1)} %cot.3, bf16[4,1792,256]{2,1,0:T(8,128)(2,1)} %pad_maximum_fusion.1.conv_w), custom_call_target="tpu_custom_call" | custom-call | tf_op jit(solution)/shard_map/spread/pallas_call | solution.py:270
  200.6 97.4 %all-reduce.10.cloned.1.call-done = (f32[128,512]{1,0:T(8,128)}, f32[128,512]{1,0:T(8,128)}) async-done(((f32[128,512]{1,0:T(8,128)}, f32[128,512]{1,0:T(8,128)}), (f32[128,512]{1,0:T(8,128)}, f32[128,512]{1,0:T(8,128)})) %all-reduce.10.cloned.1.call-update) | async-done | bytes 524304 | tf_op jit(solution)/shard_map/psum | solution.py:268
  298.1 1.1 fusion.9
  299.1 0.8 copy.24
  300.0 1.7 broadcast_multiply_fusion
  (39 shorter events, 4.4 us)
Async XLA Ops:
  7.2 290.9 %all-reduce.10.cloned.1.call-start = ((), (), s32[]{:S(2)}) async-start(), calls=%async_computation | async-start | bytes 1048576 | tf_op jit(solution)/shard_map/psum | solution.py:268
  8.1 22.0 %collective-permute-start = (bf16[3,64,128]{2,1,0:T(8,128)(2,1)S(1)}, bf16[3,64,128]{2,1,0:T(8,128)(2,1)S(1)}, u32[]{:S(2)}, u32[]{:S(2)}) collective-permute-start(bf16[3,64,128]{2,1,0:T(8,128)(2,1)S(1)} %get-tuple-element.44), channel_id=1, source_target_pairs={{0,4},{4,8},{8,12},{12,16},{16,20},{20,24},{24,28},{28,0},{1,5},{5... | collective-permute-start | bytes 147464 | tf_op jit(solution)/shard_map/ppermute | solution.py:28
  11.1 19.3 %collective-permute-start.1 = (bf16[3,64,128]{2,1,0:T(8,128)(2,1)S(1)}, bf16[3,64,128]{2,1,0:T(8,128)(2,1)S(1)}, u32[]{:S(2)}, u32[]{:S(2)}) collective-permute-start(bf16[3,64,128]{2,1,0:T(8,128)(2,1)S(1)} %get-tuple-element.43), channel_id=1, source_target_pairs={{4,0},{8,4},{12,8},{16,12},{20,16},{24,20},{28,24},{0,28},{5,1},{9... | collective-permute-start | bytes 147464 | tf_op jit(solution)/shard_map/ppermute | solution.py:30
  26.5 2.1 copy-start.2
  26.5 2.8 copy-start.1
  26.5 3.5 %copy-start = (bf16[128,64,128]{2,1,0:T(8,128)(2,1)S(1)}, bf16[128,64,128]{2,1,0:T(8,128)(2,1)}, u32[]{:S(2)}) copy-start(bf16[128,64,128]{2,1,0:T(8,128)(2,1)} %param.11) | copy-start | bytes 6291460
  30.5 4.5 %collective-permute-start.2 = (bf16[134,3,128]{2,1,0:T(4,128)(2,1)S(1)}, bf16[134,3,128]{2,1,0:T(4,128)(2,1)S(1)}, u32[]{:S(2)}, u32[]{:S(2)}) collective-permute-start(bf16[134,3,128]{2,1,0:T(4,128)(2,1)S(1)} %get-tuple-element.39), channel_id=1, source_target_pairs={{0,1},{1,2},{2,3},{3,0},{4,5},{5,6},{6,7},{7,4},{8,9},{9,10},{10,1... | collective-permute-start | bytes 308744 | tf_op jit(solution)/shard_map/ppermute | solution.py:28
  30.6 5.0 %collective-permute-start.3 = (bf16[134,3,128]{2,1,0:T(4,128)(2,1)S(1)}, bf16[134,3,128]{2,1,0:T(4,128)(2,1)S(1)}, u32[]{:S(2)}, u32[]{:S(2)}) collective-permute-start(bf16[134,3,128]{2,1,0:T(4,128)(2,1)S(1)} %get-tuple-element.40), channel_id=1, source_target_pairs={{1,0},{2,1},{3,2},{0,3},{5,4},{6,5},{7,6},{4,7},{9,8},{10,9},{11,1... | collective-permute-start | bytes 308744 | tf_op jit(solution)/shard_map/ppermute | solution.py:30
  157.2 6.9 %collective-permute-start.4 = (bf16[3,64,128]{2,1,0:T(8,128)(2,1)S(1)}, bf16[3,64,128]{2,1,0:T(8,128)(2,1)S(1)}, u32[]{:S(2)}, u32[]{:S(2)}) collective-permute-start(bf16[3,64,128]{2,1,0:T(8,128)(2,1)S(1)} %get-tuple-element.42), channel_id=1, source_target_pairs={{0,4},{4,8},{8,12},{12,16},{16,20},{20,24},{24,28},{28,0},{1,5},{5... | collective-permute-start | bytes 147464 | tf_op jit(solution)/shard_map/ppermute | solution.py:28
  160.0 6.0 %collective-permute-start.5 = (bf16[3,64,128]{2,1,0:T(8,128)(2,1)S(1)}, bf16[3,64,128]{2,1,0:T(8,128)(2,1)S(1)}, u32[]{:S(2)}, u32[]{:S(2)}) collective-permute-start(bf16[3,64,128]{2,1,0:T(8,128)(2,1)S(1)} %get-tuple-element.41), channel_id=1, source_target_pairs={{4,0},{8,4},{12,8},{16,12},{20,16},{24,20},{28,24},{0,28},{5,1},{9... | collective-permute-start | bytes 147464 | tf_op jit(solution)/shard_map/ppermute | solution.py:30
  166.1 4.5 %collective-permute-start.6 = (bf16[134,3,128]{2,1,0:T(4,128)(2,1)S(1)}, bf16[134,3,128]{2,1,0:T(4,128)(2,1)S(1)}, u32[]{:S(2)}, u32[]{:S(2)}) collective-permute-start(bf16[134,3,128]{2,1,0:T(4,128)(2,1)S(1)} %get-tuple-element.37), channel_id=1, source_target_pairs={{0,1},{1,2},{2,3},{3,0},{4,5},{5,6},{6,7},{7,4},{8,9},{9,10},{10,1... | collective-permute-start | bytes 308744 | tf_op jit(solution)/shard_map/ppermute | solution.py:28
  166.2 5.6 %collective-permute-start.7 = (bf16[134,3,128]{2,1,0:T(4,128)(2,1)S(1)}, bf16[134,3,128]{2,1,0:T(4,128)(2,1)S(1)}, u32[]{:S(2)}, u32[]{:S(2)}) collective-permute-start(bf16[134,3,128]{2,1,0:T(4,128)(2,1)S(1)} %get-tuple-element.38), channel_id=1, source_target_pairs={{1,0},{2,1},{3,2},{0,3},{5,4},{6,5},{7,6},{4,7},{9,8},{10,9},{11,1... | collective-permute-start | bytes 308744 | tf_op jit(solution)/shard_map/ppermute | solution.py:30
  175.4 126.2 %copy-start.3 = (f32[128]{0:T(128)S(1)}, f32[128]{0:T(128)}, u32[]{:S(2)}) copy-start(f32[128]{0:T(128)} %param.20) | copy-start | bytes 1540
Sparse Core Ops, SparseCore 0:
  169.3 128.7 all-reduce.9
where the time goes:
time: 309 us
  waiting for transfers between devices  105 us (34%)
  Pallas kernels  103 us (33%)
  blocking collectives  38.9 us (13%)
  other arithmetic  20.4 us (7%)
  starting transfers between devices  14.5 us (5%)
  between operations  14.2 us (5%)
  local copies, waits for them, and re-layouts  12.8 us (4%)
    psum x1, waiting for transfers between devices, local(): sums = lax.psum((g_up, g_dn, g_bup, g_small, g_kern), ('gx', 'gy'))  97.4 us
    pallas_call x1, Pallas kernels, local(): pl.pallas_call(functools.partial(forward_back, taps, count), out_shape=[s...  78 us
    psum x1, blocking collectives, local(): sums = lax.psum((g_up, g_dn, g_bup, g_small, g_kern), ('gx', 'gy'))  38.9 us
    pallas_call x1, Pallas kernels, local(): pl.pallas_call(functools.partial(spread_kernel, taps, count), out_shape=s...  25.2 us
    ppermute x4, starting transfers between devices, extended(): lax.ppermute(head, axis, [((i + 1) % count, i) for i in range(count)])  9.04 us
    concatenate x2, other arithmetic, tap_weights(): jnp.concatenate([top, low], 1).reshape(taps * 2 * chans, 2 * chans)  6.27 us
  transfers between devices with their start and end apart: 9, of which 6 were waited for; matrix products, arithmetic and copies ran while one was open for 8% of the time, Pallas kernels for 8%

commit v1 on v0

--- a/solution.py
+++ b/solution.py
@@ -101,14 +101,14 @@
     b_up,
     w_dn_t,
     d_conv,
+    packed,
+    wide,
+    shifted,
+    d_turned,
     g_up,
     g_dn,
     g_bup,
     g_small,
-    g_kern,
-    wide,
-    shifted,
-    d_turned,
 ):
     rows, cols, chans = cot.shape
     half = count * cols
@@ -186,14 +186,65 @@
                         line = jnp.sum(block * eye, axis=0, keepdims=True)
                         lines[a] = line if lines[a] is None else lines[a] + line
         lines[taps] = jnp.zeros((1, chans), F32)
-        g_kern[b] = jnp.concatenate(lines, 0)
+        at = pl.multiple_of(b * (taps + 1), taps + 1)
+        packed[pl.ds(at, taps + 1)] = jnp.concatenate(lines, 0)
         return carry
 
     lax.fori_loop(0, taps, tap, 0)
-
-
-def spread_kernel(taps, count, padded, cot, conv_w, out, wide, shifted):
+    at = taps * (taps + 1)
+    blocks = g_up.shape[1] // chans
+    for kept in (g_up, g_dn):
+        for k in range(blocks):
+            packed[at : at + chans] = kept[:, k * chans : (k + 1) * chans]
+            at += chans
+    packed[at : at + 8] = g_small[...]
+    at += 8
+    packed[at : at + 8] = jnp.concatenate(
+        [g_bup[:, k * chans : (k + 1) * chans] for k in range(blocks)]
+        + [jnp.zeros((8 - blocks, chans), F32)],
+        0,
+    )
+    at += 8
+    packed[at:] = jnp.zeros((packed.shape[0] - at, chans), F32)
+
+
+def spread_kernel(
+    taps, count, nx, ny, padded, cot, conv_w, packed, out, total,
+    wide, shifted, got_y, part_y, got_x, whole, s1, r1, s2, r2, s3, r3, s4, r4,
+):
     rows, cols, chans = cot.shape
+    here_x, here_y = lax.axis_index("gx"), lax.axis_index("gy")
+    part = packed.shape[0] // (nx * ny)
+    block = part * nx
+    others_x = [lax.rem(here_x + d, nx) for d in range(1, nx)]
+    others_y = [lax.rem(here_y + d, ny) for d in range(1, ny)]
+
+    def span(index, size):
+        return pl.ds(pl.multiple_of(index * size, 8), size)
+
+    def send(src, dst, sent, came, there):
+        return pltpu.make_async_remote_copy(
+            src_ref=src, dst_ref=dst, send_sem=sent, recv_sem=came,
+            device_id=there, device_id_type=pl.DeviceIdType.MESH,
+        )
+
+    barrier = pltpu.get_barrier_semaphore()
+    for x in others_x:
+        pl.semaphore_signal(
+            barrier, inc=1, device_id=(x, here_y), device_id_type=pl.DeviceIdType.MESH
+        )
+    for y in others_y:
+        pl.semaphore_signal(
+            barrier, inc=1, device_id=(here_x, y), device_id_type=pl.DeviceIdType.MESH
+        )
+    pl.semaphore_wait(barrier, nx + ny - 2)
+
+    scatter_y = [
+        send(packed.at[span(y, block)], got_y.at[d], s1.at[d], r1.at[d], (here_x, y))
+        for d, y in enumerate(others_y)
+    ]
+    for copy in scatter_y:
+        copy.start()
     spread_taps(padded, wide, shifted, taps)
 
     def chunk(i, carry):
@@ -202,11 +253,55 @@
         for p in range(2):
             for k in range(count):
                 row = 2 * (first + k) + p
-                part = pair_out[k * cols : (k + 1) * cols, p * chans : (p + 1) * chans]
-                out[row] = (cot[row].astype(F32) + part).astype(BF16)
+                part_out = pair_out[k * cols : (k + 1) * cols, p * chans : (p + 1) * chans]
+                out[row] = (cot[row].astype(F32) + part_out).astype(BF16)
         return carry
 
-    lax.fori_loop(0, rows // (2 * count), chunk, 0)
+    chunks = rows // (2 * count)
+    lax.fori_loop(0, chunks // 4, chunk, 0)
+
+    for copy in scatter_y:
+        copy.wait()
+    mine = packed[span(here_y, block), :]
+    for d in range(ny - 1):
+        mine = mine + got_y[d]
+    part_y[...] = mine
+    scatter_x = [
+        send(part_y.at[span(x, part)], got_x.at[d], s2.at[d], r2.at[d], (x, here_y))
+        for d, x in enumerate(others_x)
+    ]
+    for copy in scatter_x:
+        copy.start()
+    lax.fori_loop(chunks // 4, chunks // 2, chunk, 0)
+
+    for copy in scatter_x:
+        copy.wait()
+    mine = part_y[span(here_x, part), :]
+    for d in range(nx - 1):
+        mine = mine + got_x[d]
+    own = span(here_y * nx + here_x, part)
+    whole[own, :] = mine
+    gather_x = [
+        send(whole.at[own], whole.at[own], s3.at[d], r3.at[d], (x, here_y))
+        for d, x in enumerate(others_x)
+    ]
+    for copy in gather_x:
+        copy.start()
+    lax.fori_loop(chunks // 2, 3 * chunks // 4, chunk, 0)
+
+    for copy in gather_x:
+        copy.wait()
+    own = span(here_y, block)
+    gather_y = [
+        send(whole.at[own], whole.at[own], s4.at[d], r4.at[d], (here_x, y))
+        for d, y in enumerate(others_y)
+    ]
+    for copy in gather_y:
+        copy.start()
+    lax.fori_loop(3 * chunks // 4, chunks, chunk, 0)
+    for copy in gather_y:
+        copy.wait()
+    total[...] = whole[...]
 
 
 def local(
@@ -237,20 +332,27 @@
     params = pltpu.CompilerParams(vmem_limit_bytes=VMEM_BYTES)
     count = 4
     scaled_down = (w_down.T.astype(F32) * layer_scale[:, None]).astype(BF16)
+    nx, ny = lax.axis_size("gx"), lax.axis_size("gy")
+    blocks = units // chans
+    used = taps * (taps + 1) + 2 * blocks * chans + 16
+    part = -(-used // (nx * ny * 8)) * 8
     with jax.named_scope("forward_back"):
-        d_conv, g_up, g_dn, g_bup, g_small, g_kern = pl.pallas_call(
+        d_conv, packed = pl.pallas_call(
             functools.partial(forward_back, taps, count),
             out_shape=[
                 shapes((rows, cols, chans), BF16),
-                shapes((chans, units), F32),
-                shapes((chans, units), F32),
-                shapes((1, units), F32),
-                shapes((8, chans), F32),
-                shapes((taps, taps + 1, chans), F32),
+                shapes((part * nx * ny, chans), F32),
             ],
             in_specs=[vmem] * 10,
-            out_specs=[vmem] * 6,
-            scratch_shapes=scratch + [pltpu.VMEM((2 * chans, rows * cols // 2), BF16)],
+            out_specs=[vmem] * 2,
+            scratch_shapes=scratch
+            + [
+                pltpu.VMEM((2 * chans, rows * cols // 2), BF16),
+                pltpu.VMEM((chans, units), F32),
+                pltpu.VMEM((chans, units), F32),
+                pltpu.VMEM((1, units), F32),
+                pltpu.VMEM((8, chans), F32),
+            ],
             compiler_params=params,
         )(
             padded_x,
@@ -265,30 +367,53 @@
             scaled_down,
         )
     padded_d = widened(d_conv, reach)
-    sums = lax.psum((g_up, g_dn, g_bup, g_small, g_kern), ("gx", "gy"))
+    sems = pltpu.SemaphoreType.DMA
     with jax.named_scope("spread"):
-        d_features = pl.pallas_call(
-            functools.partial(spread_kernel, taps, count),
-            out_shape=shapes((rows, cols, chans), BF16),
-            in_specs=[vmem] * 3,
-            out_specs=vmem,
-            scratch_shapes=scratch,
-            compiler_params=params,
-        )(padded_d, cotangent, tap_weights(kernel[::-1, ::-1]))
-    factor = 1.0 / math.sqrt(rows * cols * lax.axis_size("gx") * lax.axis_size("gy"))
-    g_up, g_dn, g_bup, g_small, g_kern = [entry * factor for entry in sums]
-    d_wdown = g_dn.T * layer_scale
+        d_features, summed = pl.pallas_call(
+            functools.partial(spread_kernel, taps, count, nx, ny),
+            out_shape=[
+                shapes((rows, cols, chans), BF16),
+                shapes((part * nx * ny, chans), F32),
+            ],
+            in_specs=[vmem] * 4,
+            out_specs=[vmem] * 2,
+            scratch_shapes=scratch
+            + [
+                pltpu.VMEM((ny - 1, part * nx, chans), F32),
+                pltpu.VMEM((part * nx, chans), F32),
+                pltpu.VMEM((nx - 1, part, chans), F32),
+                pltpu.VMEM((part * nx * ny, chans), F32),
+            ]
+            + [sems((ny - 1,))] * 2
+            + [sems((nx - 1,))] * 4
+            + [sems((ny - 1,))] * 2,
+            compiler_params=pltpu.CompilerParams(
+                vmem_limit_bytes=VMEM_BYTES, collective_id=0, has_side_effects=True
+            ),
+        )(padded_d, cotangent, tap_weights(kernel[::-1, ::-1]), packed)
+    factor = 1.0 / math.sqrt(rows * cols * nx * ny)
+    summed = summed * factor
+    at = taps * (taps + 1)
+    g_kern = summed[:at].reshape(taps, taps + 1, chans)
+    spans = blocks * chans
+    g_up = jnp.swapaxes(summed[at : at + spans].reshape(blocks, chans, chans), 0, 1)
+    at += spans
+    g_dn_t = jnp.swapaxes(summed[at : at + spans].reshape(blocks, chans, chans), 1, 2)
+    g_dn_t = g_dn_t.reshape(units, chans)
+    at += spans
+    g_small = summed[at : at + 8]
+    g_bup = summed[at + 8 : at + 8 + blocks].reshape(units)
     cot_sum = g_small[3]
-    d_lscale = jnp.sum(g_dn.T * w_down.astype(F32), axis=0) + b_down * cot_sum
+    d_lscale = jnp.sum(g_dn_t * w_down.astype(F32), axis=0) + b_down * cot_sum
     return (
         d_features,
         jnp.swapaxes(g_kern[:, :taps], 0, 1),
         g_small[0],
         g_small[1],
         g_small[2],
-        g_up,
-        g_bup[0],
-        d_wdown,
+        g_up.reshape(chans, units),
+        g_bup,
+        g_dn_t * layer_scale,
         layer_scale * cot_sum,
         d_lscale,
     )

time: 309 us -> 171 us (0.55)
  waiting for transfers between devices: 105 us -> 9.91 us
  blocking collectives: 38.9 us -> 0 us
  between operations: 14.2 us -> 0.86 us
  Pallas kernels: 103 us -> 113 us
    psum x1 -> x0, waiting for transfers between devices: 97.4 us -> none  [local(): sums = lax.psum((g_up, g_dn, g_bup, g_small, g_kern), ('gx', 'gy'))]
    psum x1 -> x0, blocking collectives: 38.9 us -> none  [local(): sums = lax.psum((g_up, g_dn, g_bup, g_small, g_kern), ('gx', 'gy'))]
    pallas_call x1, Pallas kernels: 25.2 us -> 35 us  [local(): pl.pallas_call(functools.partial(spread_kernel, taps, count, nx, ny), out...]
    ppermute x4, waiting for transfers between devices: 1.69 us -> 6.12 us  [extended(): lax.ppermute(head, axis, [((i + 1) % count, i) for i in range(count)])]
  transfers between devices with their start and end apart: 9 -> 8, of which waited for: 6 -> 5; matrix products, arithmetic and copies ran while one was open for 8% -> 10% of each run, Pallas kernels for 8% -> 0%
where the time goes in v1:
time: 171 us; the launch traced here: 170 us
  Pallas kernels  113 us (66%)
  other arithmetic  19.3 us (11%)
  local copies, waits for them, and re-layouts  14 us (8%)
  starting transfers between devices  12.3 us (7%)
  waiting for transfers between devices  9.91 us (6%)
    pallas_call x1, Pallas kernels, local(): pl.pallas_call(functools.partial(forward_back, taps, count), out_shape=[s...  78.3 us
    pallas_call x1, Pallas kernels, local(): pl.pallas_call(functools.partial(spread_kernel, taps, count, nx, ny), out...  35 us
    ppermute x4, starting transfers between devices, extended(): lax.ppermute(head, axis, [((i + 1) % count, i) for i in range(count)])  8.6 us
    concatenate x2, other arithmetic, tap_weights(): jnp.concatenate([top, low], 1).reshape(taps * 2 * chans, 2 * chans)  6.27 us
    ppermute x4, waiting for transfers between devices, extended(): lax.ppermute(head, axis, [((i + 1) % count, i) for i in range(count)])  6.12 us
    unnamed x27, local copies, waits for them, and re-layouts  5.19 us
    pad x2, local copies, waits for them, and re-layouts, widened(): return jnp.pad(padded, ((0, 0), (0, extra), (0, 0)))  4.09 us
    another operation x2, other arithmetic, tap_weights(): return jnp.stack(blocks).astype(BF16)  4.02 us
  transfers between devices with their start and end apart: 8, of which 5 were waited for; matrix products, arithmetic and copies ran while one was open for 10% of the time, Pallas kernels for 0%

profile of v1, /device:TPU:0, one launch (start us, length us, event | category | flops | bytes accessed | tf_op | source)
XLA Modules:
  0.0 169.6 jit_solution(15933713406895296710)
XLA Ops:
  0.6 0.8 fusion.16
  1.5 3.0 %collective-permute-start = (bf16[3,64,128]{2,1,0:T(8,128)(2,1)S(1)}, bf16[3,64,128]{2,1,0:T(8,128)(2,1)S(1)}, u32[]{:S(2)}, u32[]{:S(2)}) collective-permute-start(bf16[3,64,128]{2,1,0:T(8,128)(2,1)S(1)} %get-tuple-element.35), channel_id=1, source_target_pairs={{0,4},{4,8},{8,12},{12,16},{16,20},{20,24},{24,28},{28,0},{1,5},{5... | collective-permute-start | bytes 147464 | tf_op jit(solution)/shard_map/ppermute | solution.py:28
  4.5 3.1 %collective-permute-start.1 = (bf16[3,64,128]{2,1,0:T(8,128)(2,1)S(1)}, bf16[3,64,128]{2,1,0:T(8,128)(2,1)S(1)}, u32[]{:S(2)}, u32[]{:S(2)}) collective-permute-start(bf16[3,64,128]{2,1,0:T(8,128)(2,1)S(1)} %get-tuple-element.34), channel_id=1, source_target_pairs={{4,0},{8,4},{12,8},{16,12},{20,16},{24,20},{28,24},{0,28},{5,1},{9... | collective-permute-start | bytes 147464 | tf_op jit(solution)/shard_map/ppermute | solution.py:30
  7.6 0.8 fusion.18
  8.5 1.0 copy.22
  9.5 2.9 %multiply_convert_fusion.6 = (bf16[7,128,128]{2,1,0:T(8,128)(2,1)S(1)}, bf16[7,128,128]{2,1,0:T(8,128)(2,1)S(1)}, bf16[7,128,128]{2,1,0:T(8,128)(2,1)S(1)}, bf16...) fusion(f32[7,128]{1,0:T(8,128)S(1)} %bitcast.84, ...), kind=kLoop, calls=%fused_computation.24 | loop fusion | flops 3211264 | bytes 3326976 | tf_op jit(solution)/shard_map/convert.30
  12.4 3.1 %fusion.4 = (bf16[7,256,256]{2,1,0:T(8,128)(2,1)S(1)}, bf16[7,256,256]{2,1,0:T(8,128)(2,1)S(1)}, bf16[7,256,256]{2,1,0:T(8,128)(2,1)S(1)}, bf16[7,256,256]{2,1,0:T(8,128)(2,1)S(1)}) fusion(bf16[7,128,128]{2,1,0:T(8,128)(2,1)S(1)} %get-tuple-element.66, bf16[7,128,128]{2,1,0:T(8,128)(2,1)S(1)} %get-tuple-element.54, ...), kind=kLoop, calls=%fused_computation.10 | loop fusion | flops 14680064 | bytes 5275648 | tf_op jit(solution)/shard_map/forward_back/concatenate | solution.py:61
  15.6 2.0 %pad_maximum_fusion.conv_w = bf16[4,1792,256]{2,1,0:T(8,128)(2,1)} fusion(bf16[1,1792,256]{2,1,0:T(8,128)(2,1)S(1)} %bitcast.77, bf16[1,1792,256]{2,1,0:T(8,128)(2,1)S(1)} %bitcast.76, bf16[1,1792,256]{2,1,0:T(8,128)(2,1)S(1)} %bitcast.75, bf16[1,1792,256]{2,1,0:T(8,128)(2,1)S(1)} %bitcast.74), kind=kLoop, calls=%fused_computation | loop fusion | flops 5505024 | bytes 7340032 | tf_op jit(solution)/shard_map/forward_back/stack | solution.py:62
  17.6 0.7 fusion.10.w_dn_t
  18.4 0.8 copy.21
  19.6 0.7 collective-permute-start.3
  20.3 3.7 %collective-permute-done.3 = bf16[134,3,128]{2,1,0:T(4,128)(2,1)S(1)} collective-permute-done((bf16[134,3,128]{2,1,0:T(4,128)(2,1)S(1)}, bf16[134,3,128]{2,1,0:T(4,128)(2,1)S(1)}, u32[]{:S(2)}, u32[]{:S(2)}) %collective-permute-start.3) | collective-permute-done | bytes 102944 | tf_op jit(solution)/shard_map/ppermute | solution.py:30
  24.0 1.8 %collective-permute-done.2 = bf16[134,3,128]{2,1,0:T(4,128)(2,1)S(1)} collective-permute-done((bf16[134,3,128]{2,1,0:T(4,128)(2,1)S(1)}, bf16[134,3,128]{2,1,0:T(4,128)(2,1)S(1)}, u32[]{:S(2)}, u32[]{:S(2)}) %collective-permute-start.2) | collective-permute-done | bytes 102944 | tf_op jit(solution)/shard_map/ppermute | solution.py:28
  25.7 1.7 maximum_select_fusion
  27.4 2.0 %pad.18.padded = bf16[134,80,128]{2,1,0:T(8,128)(2,1)} pad(bf16[134,70,128]{2,1,0:T(8,128)(2,1)S(1)} %maximum_select_fusion, bf16[]{:T(256)} %constant.21.clone.1), padding=0_0x0_10x0_0 | pad | bytes 5145602 | tf_op jit(solution)/shard_map/jit(_pad)/pad | solution.py:49
  29.5 78.3 %forward_back.1 = (bf16[128,64,128]{2,1,0:T(8,128)(2,1)}, f32[1280,128]{1,0:T(8,128)}) custom-call(bf16[134,80,128]{2,1,0:T(8,128)(2,1)} %pad.18.padded, bf16[128,64,128]{2,1,0:T(8,128)(2,1)} %cot.3, bf16[4,1792,256]{2,1,0:T(8,128)(2,1)} %pad_maximum_fusion.conv_w, f32[1,128]{1,0:T(1,128)} %bitcast.92, f32[1,128]{1,0:T(1,128)} %bitcast.93, ...), custom_call_target="tpu_custom_call" | custom-call | tf_op jit(solution)/shard_map/forward_back/pallas_call | solution.py:340
  107.8 0.8 fusion.15
  108.9 3.2 %fusion.5 = (bf16[7,256,256]{2,1,0:T(8,128)(2,1)S(1)}, bf16[7,256,256]{2,1,0:T(8,128)(2,1)S(1)}, bf16[7,256,256]{2,1,0:T(8,128)(2,1)S(1)}, bf16[7,256,256]{2,1,0:T(8,128)(2,1)S(1)}) fusion(bf16[7,128,128]{2,1,0:T(8,128)(2,1)S(1)} %get-tuple-element.53, bf16[7,128,128]{2,1,0:T(8,128)(2,1)S(1)} %get-tuple-element.60, ...), kind=kLoop, calls=%fused_computation.11 | loop fusion | flops 14680064 | bytes 5275648 | tf_op jit(solution)/shard_map/spread/concatenate | solution.py:61
  112.0 4.7 %collective-permute-start.5 = (bf16[3,64,128]{2,1,0:T(8,128)(2,1)S(1)}, bf16[3,64,128]{2,1,0:T(8,128)(2,1)S(1)}, u32[]{:S(2)}, u32[]{:S(2)}) collective-permute-start(bf16[3,64,128]{2,1,0:T(8,128)(2,1)S(1)} %get-tuple-element.32), channel_id=1, source_target_pairs={{4,0},{8,4},{12,8},{16,12},{20,16},{24,20},{28,24},{0,28},{5,1},{9... | collective-permute-start | bytes 147464 | tf_op jit(solution)/shard_map/ppermute | solution.py:30
  117.1 1.4 collective-permute-done.5
  119.2 2.0 %pad_maximum_fusion.1.conv_w = bf16[4,1792,256]{2,1,0:T(8,128)(2,1)} fusion(bf16[1,1792,256]{2,1,0:T(8,128)(2,1)S(1)} %bitcast.73, bf16[1,1792,256]{2,1,0:T(8,128)(2,1)S(1)} %bitcast.72, bf16[1,1792,256]{2,1,0:T(8,128)(2,1)S(1)} %bitcast.71, bf16[1,1792,256]{2,1,0:T(8,128)(2,1)S(1)} %bitcast.70), kind=kLoop, calls=%fused_computation.1 | loop fusion | flops 5505024 | bytes 7340032 | tf_op jit(solution)/shard_map/spread/stack | solution.py:62
  121.2 1.0 collective-permute-done.7
  122.2 2.0 %collective-permute-done.6 = bf16[134,3,128]{2,1,0:T(4,128)(2,1)S(1)} collective-permute-done((bf16[134,3,128]{2,1,0:T(4,128)(2,1)S(1)}, bf16[134,3,128]{2,1,0:T(4,128)(2,1)S(1)}, u32[]{:S(2)}, u32[]{:S(2)}) %collective-permute-start.6) | collective-permute-done | bytes 102944 | tf_op jit(solution)/shard_map/ppermute | solution.py:28
  124.3 1.7 maximum_select_fusion.1
  125.9 2.0 %pad.19.padded = bf16[134,80,128]{2,1,0:T(8,128)(2,1)} pad(bf16[134,70,128]{2,1,0:T(8,128)(2,1)S(1)} %maximum_select_fusion.1, bf16[]{:T(256)} %constant.21.clone.1), padding=0_0x0_10x0_0 | pad | bytes 5145602 | tf_op jit(solution)/shard_map/jit(_pad)/pad | solution.py:49
  128.0 35.0 %spread.1 = (bf16[128,64,128]{2,1,0:T(8,128)(2,1)}, f32[1280,128]{1,0:T(8,128)}) custom-call(bf16[134,80,128]{2,1,0:T(8,128)(2,1)} %pad.19.padded, bf16[128,64,128]{2,1,0:T(8,128)(2,1)} %cot.3, bf16[4,1792,256]{2,1,0:T(8,128)(2,1)} %pad_maximum_fusion.1.conv_w, f32[1280,128]{1,0:T(8,128)} %get-tuple-element.15.packed), custom_call_target="tpu_custom_call" | custom-call | tf_op jit(solution)/shard_map/spread/pallas_call | solution.py:372
  163.0 1.3 broadcast_multiply_fusion
  164.9 0.6 slice_bitcast_fusion.1
  165.5 0.6 copy.35
  166.1 0.7 copy.34
  166.9 0.8 copy.26
  168.3 1.3 copy.41
  (47 shorter events, 3.0 us)
Async XLA Ops:
  1.5 17.7 %collective-permute-start = (bf16[3,64,128]{2,1,0:T(8,128)(2,1)S(1)}, bf16[3,64,128]{2,1,0:T(8,128)(2,1)S(1)}, u32[]{:S(2)}, u32[]{:S(2)}) collective-permute-start(bf16[3,64,128]{2,1,0:T(8,128)(2,1)S(1)} %get-tuple-element.35), channel_id=1, source_target_pairs={{0,4},{4,8},{8,12},{12,16},{16,20},{20,24},{24,28},{28,0},{1,5},{5... | collective-permute-start | bytes 147464 | tf_op jit(solution)/shard_map/ppermute | solution.py:28
  4.5 15.0 %collective-permute-start.1 = (bf16[3,64,128]{2,1,0:T(8,128)(2,1)S(1)}, bf16[3,64,128]{2,1,0:T(8,128)(2,1)S(1)}, u32[]{:S(2)}, u32[]{:S(2)}) collective-permute-start(bf16[3,64,128]{2,1,0:T(8,128)(2,1)S(1)} %get-tuple-element.34), channel_id=1, source_target_pairs={{4,0},{8,4},{12,8},{16,12},{20,16},{24,20},{28,24},{0,28},{5,1},{9... | collective-permute-start | bytes 147464 | tf_op jit(solution)/shard_map/ppermute | solution.py:30
  15.6 2.1 %copy-start.7 = (f32[128]{0:T(128)S(1)}, f32[128]{0:T(128)}, u32[]{:S(2)}) copy-start(f32[128]{0:T(128)} %param.21) | copy-start | bytes 1540
  15.6 2.8 %copy-start.6 = (bf16[128,512]{1,0:T(8,128)(2,1)S(1)}, bf16[128,512]{1,0:T(8,128)(2,1)}, u32[]{:S(2)}) copy-start(bf16[128,512]{1,0:T(8,128)(2,1)} %w_up.1) | copy-start | bytes 393220
  15.6 3.6 %copy-start = (bf16[128,64,128]{2,1,0:T(8,128)(2,1)S(1)}, bf16[128,64,128]{2,1,0:T(8,128)(2,1)}, u32[]{:S(2)}) copy-start(bf16[128,64,128]{2,1,0:T(8,128)(2,1)} %param.11) | copy-start | bytes 6291460
  19.6 4.4 %collective-permute-start.3 = (bf16[134,3,128]{2,1,0:T(4,128)(2,1)S(1)}, bf16[134,3,128]{2,1,0:T(4,128)(2,1)S(1)}, u32[]{:S(2)}, u32[]{:S(2)}) collective-permute-start(bf16[134,3,128]{2,1,0:T(4,128)(2,1)S(1)} %get-tuple-element.31), channel_id=1, source_target_pairs={{1,0},{2,1},{3,2},{0,3},{5,4},{6,5},{7,6},{4,7},{9,8},{10,9},{11,1... | collective-permute-start | bytes 308744 | tf_op jit(solution)/shard_map/ppermute | solution.py:30
  20.3 5.4 %collective-permute-start.2 = (bf16[134,3,128]{2,1,0:T(4,128)(2,1)S(1)}, bf16[134,3,128]{2,1,0:T(4,128)(2,1)S(1)}, u32[]{:S(2)}, u32[]{:S(2)}) collective-permute-start(bf16[134,3,128]{2,1,0:T(4,128)(2,1)S(1)} %get-tuple-element.30), channel_id=1, source_target_pairs={{0,1},{1,2},{2,3},{3,0},{4,5},{5,6},{6,7},{7,4},{8,9},{9,10},{10,1... | collective-permute-start | bytes 308744 | tf_op jit(solution)/shard_map/ppermute | solution.py:28
  29.5 79.4 %copy-start.3 = (bf16[7,128,128]{2,1,0:T(8,128)(2,1)S(1)}, bf16[7,128,128]{2,1,0:T(8,128)(2,1)}, u32[]{:S(2)}) copy-start(bf16[7,128,128]{2,1,0:T(8,128)(2,1)} %get-tuple-element.63) | copy-start | bytes 688132
  29.5 79.4 %copy-start.4 = (bf16[7,128,128]{2,1,0:T(8,128)(2,1)S(1)}, bf16[7,128,128]{2,1,0:T(8,128)(2,1)}, u32[]{:S(2)}) copy-start(bf16[7,128,128]{2,1,0:T(8,128)(2,1)} %get-tuple-element.64) | copy-start | bytes 688132
  29.5 79.4 %copy-start.5 = (bf16[7,128,128]{2,1,0:T(8,128)(2,1)S(1)}, bf16[7,128,128]{2,1,0:T(8,128)(2,1)}, u32[]{:S(2)}) copy-start(bf16[7,128,128]{2,1,0:T(8,128)(2,1)} %get-tuple-element.65) | copy-start | bytes 688132
  108.6 8.2 %collective-permute-start.4 = (bf16[3,64,128]{2,1,0:T(8,128)(2,1)S(1)}, bf16[3,64,128]{2,1,0:T(8,128)(2,1)S(1)}, u32[]{:S(2)}, u32[]{:S(2)}) collective-permute-start(bf16[3,64,128]{2,1,0:T(8,128)(2,1)S(1)} %get-tuple-element.33), channel_id=1, source_target_pairs={{0,4},{4,8},{8,12},{12,16},{16,20},{20,24},{24,28},{28,0},{1,5},{5... | collective-permute-start | bytes 147464 | tf_op jit(solution)/shard_map/ppermute | solution.py:28
  108.9 7.9 %copy-start.1 = (bf16[128,64,128]{2,1,0:T(8,128)(2,1)S(1)}, bf16[128,64,128]{2,1,0:T(8,128)(2,1)}, u32[]{:S(2)}) copy-start(bf16[128,64,128]{2,1,0:T(8,128)(2,1)} %get-tuple-element.14) | copy-start | bytes 6291460
  112.0 6.5 %collective-permute-start.5 = (bf16[3,64,128]{2,1,0:T(8,128)(2,1)S(1)}, bf16[3,64,128]{2,1,0:T(8,128)(2,1)S(1)}, u32[]{:S(2)}, u32[]{:S(2)}) collective-permute-start(bf16[3,64,128]{2,1,0:T(8,128)(2,1)S(1)} %get-tuple-element.32), channel_id=1, source_target_pairs={{4,0},{8,4},{12,8},{16,12},{20,16},{24,20},{28,24},{0,28},{5,1},{9... | collective-permute-start | bytes 147464 | tf_op jit(solution)/shard_map/ppermute | solution.py:30
  118.7 3.6 %collective-permute-start.7 = (bf16[134,3,128]{2,1,0:T(4,128)(2,1)S(1)}, bf16[134,3,128]{2,1,0:T(4,128)(2,1)S(1)}, u32[]{:S(2)}, u32[]{:S(2)}) collective-permute-start(bf16[134,3,128]{2,1,0:T(4,128)(2,1)S(1)} %get-tuple-element.29), channel_id=1, source_target_pairs={{1,0},{2,1},{3,2},{0,3},{5,4},{6,5},{7,6},{4,7},{9,8},{10,9},{11,1... | collective-permute-start | bytes 308744 | tf_op jit(solution)/shard_map/ppermute | solution.py:30
  118.7 5.5 %collective-permute-start.6 = (bf16[134,3,128]{2,1,0:T(4,128)(2,1)S(1)}, bf16[134,3,128]{2,1,0:T(4,128)(2,1)S(1)}, u32[]{:S(2)}, u32[]{:S(2)}) collective-permute-start(bf16[134,3,128]{2,1,0:T(4,128)(2,1)S(1)} %get-tuple-element.28), channel_id=1, source_target_pairs={{0,1},{1,2},{2,3},{3,0},{4,5},{5,6},{6,7},{7,4},{8,9},{9,10},{10,1... | collective-permute-start | bytes 308744 | tf_op jit(solution)/shard_map/ppermute | solution.py:28
  163.0 4.8 %copy-start.8 = (f32[128]{0:T(128)S(1)}, f32[128]{0:T(128)}, u32[]{:S(2)}) copy-start(f32[128]{0:T(128)} %param.20) | copy-start | bytes 1540
  163.0 5.3 %copy-start.2 = (bf16[128,64,128]{2,1,0:T(8,128)(2,1)S(1)}, bf16[128,64,128]{2,1,0:T(8,128)(2,1)}, u32[]{:S(2)}) copy-start(bf16[128,64,128]{2,1,0:T(8,128)(2,1)} %get-tuple-element.91) | copy-start | bytes 6291460

commit v2 on v1

--- a/solution.py
+++ b/solution.py
@@ -18,63 +18,166 @@
     return jnp.dot(left, right, preferred_element_type=F32)
 
 
-def extended(cells, sides, width):
-    for axis, dim in sides:
-        count = lax.axis_size(axis)
-        head = lax.slice_in_dim(cells, 0, width, axis=dim)
-        tail = lax.slice_in_dim(cells, cells.shape[dim] - width, cells.shape[dim], axis=dim)
-        cells = jnp.concatenate(
+def build_weights(kernel, weights, flip):
+    taps, _, chans = kernel.shape
+    keep = lax.broadcasted_iota(jnp.int32, (chans, chans), 0) == lax.broadcasted_iota(
+        jnp.int32, (chans, chans), 1
+    )
+    for q in range(weights.shape[0]):
+        for b in range(taps):
+            for s in range(2):
+                for p in range(2):
+                    a = 2 * q + s - p
+                    at = (2 * b + s) * chans
+                    if 0 <= a < taps:
+                        u, v = (taps - 1 - a, taps - 1 - b) if flip else (a, b)
+                        block = jnp.where(keep, kernel[u, v : v + 1, :], 0.0).astype(BF16)
+                    else:
+                        block = jnp.zeros((chans, chans), BF16)
+                    weights[q, at : at + chans, p * chans : (p + 1) * chans] = block
+
+
+def send(src, dst, sent, came, there):
+    return pltpu.make_async_remote_copy(
+        src_ref=src,
+        dst_ref=dst,
+        send_sem=sent,
+        recv_sem=came,
+        device_id=there,
+        device_id_type=pl.DeviceIdType.MESH,
+    )
+
+
+def greet(peers):
+    barrier = pltpu.get_barrier_semaphore()
+    for there in peers:
+        pl.semaphore_signal(
+            barrier, inc=1, device_id=there, device_id_type=pl.DeviceIdType.MESH
+        )
+    pl.semaphore_wait(barrier, len(peers))
+
+
+def around(nx, ny):
+    here_x, here_y = lax.axis_index("gx"), lax.axis_index("gy")
+    up, down = lax.rem(here_x + nx - 1, nx), lax.rem(here_x + 1, nx)
+    left, right = lax.rem(here_y + ny - 1, ny), lax.rem(here_y + 1, ny)
+    return here_x, here_y, up, down, left, right
+
+
+def pack_edges(cells, edge_out):
+    rows, cols, _ = cells.shape
+
+    def group(g, carry):
+        for side in range(2):
+            at = 0 if side == 0 else cols - 16
+            lines = [cells[4 * g + k, at : at + 16, :].astype(F32) for k in range(4)]
+            cut = slice(0, 4) if side == 0 else slice(12, 16)
+            edge_out[side, g] = jnp.concatenate([line[cut] for line in lines], 0).astype(BF16)
+        return carry
+
+    lax.fori_loop(0, rows // 4, group, 0)
+
+
+def halo_copies(nx, ny, cells, edge_out, edge_in, row_in, sent, came):
+    rows = cells.shape[0]
+    groups = rows // 4
+    here_x, here_y, up, down, left, right = around(nx, ny)
+    plain = [
+        send(cells.at[0:4], row_in.at[1], sent.at[0], came.at[0], (up, here_y)),
+        send(cells.at[rows - 4 : rows], row_in.at[0], sent.at[1], came.at[1], (down, here_y)),
+    ]
+    sides = []
+    for side, column in ((0, left), (1, right)):
+        other = 1 - side
+        base = 2 + 3 * side
+        sides.append(
             [
-                lax.ppermute(tail, axis, [(i, (i + 1) % count) for i in range(count)]),
-                cells,
-                lax.ppermute(head, axis, [((i + 1) % count, i) for i in range(count)]),
-            ],
-            axis=dim,
+                send(
+                    edge_out.at[side],
+                    edge_in.at[other, 1 : groups + 1],
+                    sent.at[base],
+                    came.at[base],
+                    (here_x, column),
+                ),
+                send(
+                    edge_out.at[side, 0],
+                    edge_in.at[other, groups + 1],
+                    sent.at[base + 1],
+                    came.at[base + 1],
+                    (up, column),
+                ),
+                send(
+                    edge_out.at[side, groups - 1],
+                    edge_in.at[other, 0],
+                    sent.at[base + 2],
+                    came.at[base + 2],
+                    (down, column),
+                ),
+            ]
         )
-    return cells
-
-
-def mask_edges(padded, width):
-    col_total = padded.shape[1]
-    inner_cols = col_total - 2 * width
-    grid_cols = inner_cols * lax.axis_size("gy")
-    col_place = lax.axis_index("gy") * inner_cols + lax.iota(jnp.int32, col_total) - width
-    keep_mask = (col_place >= 0) & (col_place < grid_cols)
-    return jnp.where(keep_mask[None, :, None], padded, jnp.zeros((), padded.dtype))
-
-
-def widened(cells, reach):
-    padded = mask_edges(extended(cells, (("gx", 0), ("gy", 1)), reach), reach)
-    extra = -padded.shape[1] % 16
-    return jnp.pad(padded, ((0, 0), (0, extra), (0, 0)))
-
-
-def tap_weights(kernel):
-    taps, _, chans = kernel.shape
-    pairs = (taps + 1) // 2
-    framed = jnp.pad(kernel, ((1, 1), (0, 0), (0, 0)))
-    eye = jnp.eye(chans, dtype=F32)
-    blocks = []
-    for q in range(pairs):
-        top = jnp.concatenate([framed[2 * q + 1, :, :, None] * eye, framed[2 * q, :, :, None] * eye], 2)
-        low = jnp.concatenate([framed[2 * q + 2, :, :, None] * eye, framed[2 * q + 1, :, :, None] * eye], 2)
-        blocks.append(jnp.concatenate([top, low], 1).reshape(taps * 2 * chans, 2 * chans))
-    return jnp.stack(blocks).astype(BF16)
-
-
-def spread_taps(padded, wide, shifted, taps):
-    pairs, cols, _ = shifted.shape
-    chans = padded.shape[2]
-
-    def one(j, carry):
-        for s in range(2):
-            wide[s] = padded[2 * j + s].astype(F32)
-            for b in range(taps):
-                at = (2 * b + s) * chans
-                shifted[j, :, at : at + chans] = wide[s, b : b + cols, :].astype(BF16)
+    return plain, sides, here_y > 0, here_y < ny - 1
+
+
+def halo_start(copies, edge_in):
+    plain, sides, has_left, has_right = copies
+    for copy in plain:
+        copy.start()
+    for side, has in ((0, has_left), (1, has_right)):
+
+        @pl.when(has)
+        def _():
+            for copy in sides[side]:
+                copy.start()
+
+        @pl.when(jnp.logical_not(has))
+        def _():
+            edge_in[side] = jnp.zeros(edge_in.shape[1:], BF16)
+
+
+def halo_wait(copies):
+    plain, sides, has_left, has_right = copies
+    for copy in plain:
+        copy.wait()
+    for side, has, back in ((0, has_left, has_right), (1, has_right, has_left)):
+
+        @pl.when(has)
+        def _():
+            for copy in sides[side]:
+                copy.wait_send()
+
+        @pl.when(back)
+        def _():
+            for copy in sides[side]:
+                copy.wait_recv()
+
+
+def spread_taps(cells, edge_in, row_in, wide, shifted, taps):
+    rows, cols, chans = cells.shape
+    groups = rows // 4
+    reach = taps // 2
+
+    def line(g, k, row):
+        wide[k, 8 : 8 + cols, :] = row.astype(F32)
+        wide[k, 4:8, :] = edge_in[0, g].astype(F32)[4 * k : 4 * k + 4]
+        wide[k, 8 + cols : 12 + cols, :] = edge_in[1, g].astype(F32)[4 * k : 4 * k + 4]
+        j = 2 * g + (k + 1) // 2 - 1
+        s = (k + 1) % 2
+        for b in range(taps):
+            at = (2 * b + s) * chans
+            start = 8 - reach + b
+            shifted[j, :, at : at + chans] = wide[k, start : start + cols, :].astype(BF16)
+
+    for k in range(1, 4):
+        line(0, k, row_in[0, k])
+
+    def one(g, carry):
+        for k in range(4):
+            line(g, k, cells[4 * (g - 1) + k])
         return carry
 
-    lax.fori_loop(0, pairs, one, 0)
+    lax.fori_loop(1, groups + 1, one, 0)
+    for k in range(3):
+        line(groups + 1, k, row_in[1, k])
 
 
 def conv_pairs(shifted, weights, first, count):
@@ -82,7 +185,7 @@
     total = None
     for q in range(weights.shape[0]):
         rows = shifted[pl.ds(first + q, count)].reshape(count * cols, depth)
-        part = dot(rows, weights[q])
+        part = dot(rows, weights[q, :, :])
         total = part if total is None else total + part
     return total
 
@@ -90,9 +193,11 @@
 def forward_back(
     taps,
     count,
-    padded,
+    nx,
+    ny,
+    cells,
     cot,
-    conv_w,
+    kernel,
     kbias,
     gain,
     shift,
@@ -109,10 +214,26 @@
     g_dn,
     g_bup,
     g_small,
+    conv_w,
+    edge_out,
+    edge_in,
+    row_in,
+    sent,
+    came,
 ):
     rows, cols, chans = cot.shape
     half = count * cols
-    spread_taps(padded, wide, shifted, taps)
+    here_x, here_y, up, down, left, right = around(nx, ny)
+    pack_edges(cells, edge_out)
+    greet(
+        [(up, here_y), (down, here_y)]
+        + [(x, y) for y in (left, right) for x in (here_x, up, down)]
+    )
+    copies = halo_copies(nx, ny, cells, edge_out, edge_in, row_in, sent, came)
+    halo_start(copies, edge_in)
+    build_weights(kernel, conv_w, False)
+    halo_wait(copies)
+    spread_taps(cells, edge_in, row_in, wide, shifted, taps)
     g_up[...] = jnp.zeros_like(g_up)
     g_dn[...] = jnp.zeros_like(g_dn)
     g_bup[...] = jnp.zeros_like(g_bup)
@@ -193,10 +314,12 @@
     lax.fori_loop(0, taps, tap, 0)
     at = taps * (taps + 1)
     blocks = g_up.shape[1] // chans
-    for kept in (g_up, g_dn):
-        for k in range(blocks):
-            packed[at : at + chans] = kept[:, k * chans : (k + 1) * chans]
-            at += chans
+    for k in range(blocks):
+        packed[at : at + chans] = g_up[:, k * chans : (k + 1) * chans]
+        at += chans
+    for k in range(blocks):
+        packed[at : at + chans] = g_dn[:, k * chans : (k + 1) * chans].T
+        at += chans
     packed[at : at + 8] = g_small[...]
     at += 8
     packed[at : at + 8] = jnp.concatenate(
@@ -209,11 +332,14 @@
 
 
 def spread_kernel(
-    taps, count, nx, ny, padded, cot, conv_w, packed, out, total,
-    wide, shifted, got_y, part_y, got_x, whole, s1, r1, s2, r2, s3, r3, s4, r4,
+    taps, count, nx, ny, factor,
+    cells, cot, kernel, packed, w_down, b_down, scale,
+    out, o_kern, o_up, o_dn, o_bup, o_small,
+    wide, shifted, got_y, part_y, got_x, whole, conv_w, edge_out, edge_in, row_in,
+    sent, came, s1, r1, s2, r2, s3, r3, s4, r4,
 ):
     rows, cols, chans = cot.shape
-    here_x, here_y = lax.axis_index("gx"), lax.axis_index("gy")
+    here_x, here_y, up, down, left, right = around(nx, ny)
     part = packed.shape[0] // (nx * ny)
     block = part * nx
     others_x = [lax.rem(here_x + d, nx) for d in range(1, nx)]
@@ -222,30 +348,23 @@
     def span(index, size):
         return pl.ds(pl.multiple_of(index * size, 8), size)
 
-    def send(src, dst, sent, came, there):
-        return pltpu.make_async_remote_copy(
-            src_ref=src, dst_ref=dst, send_sem=sent, recv_sem=came,
-            device_id=there, device_id_type=pl.DeviceIdType.MESH,
-        )
-
-    barrier = pltpu.get_barrier_semaphore()
-    for x in others_x:
-        pl.semaphore_signal(
-            barrier, inc=1, device_id=(x, here_y), device_id_type=pl.DeviceIdType.MESH
-        )
-    for y in others_y:
-        pl.semaphore_signal(
-            barrier, inc=1, device_id=(here_x, y), device_id_type=pl.DeviceIdType.MESH
-        )
-    pl.semaphore_wait(barrier, nx + ny - 2)
-
+    pack_edges(cells, edge_out)
+    greet(
+        [(x, here_y) for x in others_x]
+        + [(here_x, y) for y in others_y]
+        + [(x, y) for y in (left, right) for x in (up, down)]
+    )
+    copies = halo_copies(nx, ny, cells, edge_out, edge_in, row_in, sent, came)
+    halo_start(copies, edge_in)
     scatter_y = [
         send(packed.at[span(y, block)], got_y.at[d], s1.at[d], r1.at[d], (here_x, y))
         for d, y in enumerate(others_y)
     ]
     for copy in scatter_y:
         copy.start()
-    spread_taps(padded, wide, shifted, taps)
+    build_weights(kernel, conv_w, True)
+    halo_wait(copies)
+    spread_taps(cells, edge_in, row_in, wide, shifted, taps)
 
     def chunk(i, carry):
         first = i * count
@@ -301,7 +420,31 @@
     lax.fori_loop(3 * chunks // 4, chunks, chunk, 0)
     for copy in gather_y:
         copy.wait()
-    total[...] = whole[...]
+    at = taps * (taps + 1)
+    for b in range(taps):
+        lines = whole[b * (taps + 1) : (b + 1) * (taps + 1)] * factor
+        for a in range(taps):
+            o_kern[a, b : b + 1] = lines[a : a + 1]
+    blocks = o_up.shape[1] // chans
+    for k in range(blocks):
+        o_up[:, k * chans : (k + 1) * chans] = whole[at : at + chans] * factor
+        at += chans
+    kept = jnp.zeros((1, chans), F32)
+    for k in range(blocks):
+        grad = whole[at : at + chans] * factor
+        down_w = w_down[k * chans : (k + 1) * chans].astype(F32)
+        kept = kept + jnp.sum(grad * down_w, axis=0, keepdims=True)
+        o_dn[k * chans : (k + 1) * chans] = grad * scale[...]
+        at += chans
+    small = whole[at : at + 8] * factor
+    cot_sum = small[3:4]
+    o_small[0:3] = small[0:3]
+    o_small[3:4] = cot_sum * scale[...]
+    o_small[4:5] = kept + b_down[...] * cot_sum
+    o_small[5:8] = jnp.zeros((3, chans), F32)
+    at += 8
+    for k in range(blocks):
+        o_bup[:, k * chans : (k + 1) * chans] = whole[at + k : at + k + 1] * factor
 
 
 def local(
@@ -321,24 +464,32 @@
     reach = taps // 2
     rows, cols, chans = features.shape
     units = w_up.shape[1]
-    padded_x = widened(features, reach)
-    pairs = padded_x.shape[0] // 2
+    nx, ny = lax.axis_size("gx"), lax.axis_size("gy")
+    pairs = (rows + 2 * reach) // 2
+    groups = rows // 4
     shapes = jax.ShapeDtypeStruct
+    sems = pltpu.SemaphoreType.DMA
     scratch = [
-        pltpu.VMEM((2, padded_x.shape[1], chans), F32),
+        pltpu.VMEM((4, cols + 16, chans), F32),
         pltpu.VMEM((pairs, cols, taps * 2 * chans), BF16),
     ]
+    halo = [
+        pltpu.VMEM(((taps + 1) // 2, taps * 2 * chans, 2 * chans), BF16),
+        pltpu.VMEM((2, groups, 16, chans), BF16),
+        pltpu.VMEM((2, groups + 2, 16, chans), BF16),
+        pltpu.VMEM((2, 4, cols, chans), BF16),
+        sems((8,)),
+        sems((8,)),
+    ]
     vmem = pl.BlockSpec(memory_space=pltpu.VMEM)
-    params = pltpu.CompilerParams(vmem_limit_bytes=VMEM_BYTES)
     count = 4
     scaled_down = (w_down.T.astype(F32) * layer_scale[:, None]).astype(BF16)
-    nx, ny = lax.axis_size("gx"), lax.axis_size("gy")
     blocks = units // chans
     used = taps * (taps + 1) + 2 * blocks * chans + 16
     part = -(-used // (nx * ny * 8)) * 8
     with jax.named_scope("forward_back"):
         d_conv, packed = pl.pallas_call(
-            functools.partial(forward_back, taps, count),
+            functools.partial(forward_back, taps, count, nx, ny),
             out_shape=[
                 shapes((rows, cols, chans), BF16),
                 shapes((part * nx * ny, chans), F32),
@@ -352,12 +503,15 @@
                 pltpu.VMEM((chans, units), F32),
                 pltpu.VMEM((1, units), F32),
                 pltpu.VMEM((8, chans), F32),
-            ],
-            compiler_params=params,
+            ]
+            + halo,
+            compiler_params=pltpu.CompilerParams(
+                vmem_limit_bytes=VMEM_BYTES, collective_id=1, has_side_effects=True
+            ),
         )(
-            padded_x,
+            features,
             cotangent,
-            tap_weights(kernel),
+            kernel,
             kernel_bias[None],
             norm_gain[None],
             norm_shift[None],
@@ -366,17 +520,20 @@
             b_up[None],
             scaled_down,
         )
-    padded_d = widened(d_conv, reach)
-    sems = pltpu.SemaphoreType.DMA
+    factor = 1.0 / math.sqrt(rows * cols * nx * ny)
     with jax.named_scope("spread"):
-        d_features, summed = pl.pallas_call(
-            functools.partial(spread_kernel, taps, count, nx, ny),
+        d_features, d_kern, d_wup, d_wdown, d_bup, small = pl.pallas_call(
+            functools.partial(spread_kernel, taps, count, nx, ny, factor),
             out_shape=[
                 shapes((rows, cols, chans), BF16),
-                shapes((part * nx * ny, chans), F32),
+                shapes((taps, taps, chans), F32),
+                shapes((chans, units), F32),
+                shapes((units, chans), F32),
+                shapes((1, units), F32),
+                shapes((8, chans), F32),
             ],
-            in_specs=[vmem] * 4,
-            out_specs=[vmem] * 2,
+            in_specs=[vmem] * 7,
+            out_specs=[vmem] * 6,
             scratch_shapes=scratch
             + [
                 pltpu.VMEM((ny - 1, part * nx, chans), F32),
@@ -384,38 +541,25 @@
                 pltpu.VMEM((nx - 1, part, chans), F32),
                 pltpu.VMEM((part * nx * ny, chans), F32),
             ]
+            + halo
             + [sems((ny - 1,))] * 2
             + [sems((nx - 1,))] * 4
             + [sems((ny - 1,))] * 2,
             compiler_params=pltpu.CompilerParams(
                 vmem_limit_bytes=VMEM_BYTES, collective_id=0, has_side_effects=True
             ),
-        )(padded_d, cotangent, tap_weights(kernel[::-1, ::-1]), packed)
-    factor = 1.0 / math.sqrt(rows * cols * nx * ny)
-    summed = summed * factor
-    at = taps * (taps + 1)
-    g_kern = summed[:at].reshape(taps, taps + 1, chans)
-    spans = blocks * chans
-    g_up = jnp.swapaxes(summed[at : at + spans].reshape(blocks, chans, chans), 0, 1)
-    at += spans
-    g_dn_t = jnp.swapaxes(summed[at : at + spans].reshape(blocks, chans, chans), 1, 2)
-    g_dn_t = g_dn_t.reshape(units, chans)
-    at += spans
-    g_small = summed[at : at + 8]
-    g_bup = summed[at + 8 : at + 8 + blocks].reshape(units)
-    cot_sum = g_small[3]
-    d_lscale = jnp.sum(g_dn_t * w_down.astype(F32), axis=0) + b_down * cot_sum
+        )(d_conv, cotangent, kernel, packed, w_down, b_down[None], layer_scale[None])
     return (
         d_features,
-        jnp.swapaxes(g_kern[:, :taps], 0, 1),
-        g_small[0],
-        g_small[1],
-        g_small[2],
-        g_up.reshape(chans, units),
-        g_bup,
-        g_dn_t * layer_scale,
-        layer_scale * cot_sum,
-        d_lscale,
+        d_kern,
+        small[0],
+        small[1],
+        small[2],
+        d_wup,
+        d_bup[0],
+        d_wdown,
+        small[3],
+        small[4],
     )
 
 

time: 171 us -> 138 us (0.81)
  other arithmetic: 19.3 us -> 1.4 us
  Pallas kernels: 113 us -> 126 us
  starting transfers between devices: 12.3 us -> 0 us
  waiting for transfers between devices: 9.91 us -> 0 us
  local copies, waits for them, and re-layouts: 14 us -> 9.81 us
    pallas_call x2, Pallas kernels: 113 us -> 126 us  [the longest x1 87.5 us: local(): pl.pallas_call(functools.partial(forward_back, taps, count, nx, ny), out_...]
    ppermute x8 -> x0, starting transfers between devices: 12.3 us -> none  [the longest x4 8.6 us: extended(): lax.ppermute(head, axis, [((i + 1) % count, i) for i in range(count)])]
    ppermute x8 -> x0, waiting for transfers between devices: 9.91 us -> none  [the longest x4 6.12 us: extended(): lax.ppermute(head, axis, [((i + 1) % count, i) for i in range(count)])]
    another operation x3 -> x0, other arithmetic: 6.94 us -> none  [the longest x2 4.02 us: tap_weights(): return jnp.stack(blocks).astype(BF16)]
    concatenate x2 -> x0, other arithmetic: 6.27 us -> none  [tap_weights(): jnp.concatenate([top, low], 1).reshape(taps * 2 * chans, 2 * chans)]
    pad x2 -> x0, local copies, waits for them, and re-layouts: 4.09 us -> none  [widened(): return jnp.pad(padded, ((0, 0), (0, extra), (0, 0)))]
    select_n x2 -> x0, other arithmetic: 3.36 us -> none  [mask_edges(): jnp.where(keep_mask[None, :, None], padded, jnp.zeros((), padded.dtype))]
    unnamed x27 -> x15, local copies, waits for them, and re-layouts: 5.19 us -> 8.42 us
  transfers between devices with their start and end apart: 8 -> 0, of which waited for: 5 -> 0; matrix products, arithmetic and copies ran while one was open for 10% -> 0% of each run, Pallas kernels for 0% -> 0%
where the time goes in v2:
time: 138 us
  Pallas kernels  126 us (91%)
  local copies, waits for them, and re-layouts  9.81 us (7%)
  other arithmetic  1.4 us (1%)
    pallas_call x1, Pallas kernels, local(): pl.pallas_call(functools.partial(forward_back, taps, count, nx, ny), out_...  87.5 us
    pallas_call x1, Pallas kernels, local(): pl.pallas_call(functools.partial(spread_kernel, taps, count, nx, ny, fact...  38.2 us
    unnamed x15, local copies, waits for them, and re-layouts  8.42 us

profile of v2, /device:TPU:0, one launch (start us, length us, event | category | flops | bytes accessed | tf_op | source)
XLA Modules:
  0.0 137.6 jit_solution(12439619241454621528)
XLA Ops:
  0.6 1.7 %copy.21 = bf16[128,512]{0,1:T(8,128)(2,1)} copy(bf16[128,512]{1,0:T(8,128)(2,1)} %w_up.1) | data formatting | bytes 262144 | tf_op args[6]
  2.3 1.0 copy.22
  3.3 1.4 %fusion.w_dn_t = bf16[128,512]{1,0:T(8,128)(2,1)} fusion(bf16[512,128]{0,1:T(8,128)(2,1)S(1)} %copy.22, f32[128]{0:T(128)} %param.21), kind=kLoop, calls=%fused_computation.1 | loop fusion | flops 196608 | bytes 262656 | tf_op jit(solution)/shard_map/convert_element_type | solution.py:486
  4.7 87.5 %forward_back.1 = (bf16[128,64,128]{2,1,0:T(8,128)(2,1)}, f32[1280,128]{1,0:T(8,128)}) custom-call(bf16[128,64,128]{2,1,0:T(8,128)(2,1)} %cells.1, bf16[128,64,128]{2,1,0:T(8,128)(2,1)} %cot.3, f32[7,7,128]{2,1,0:T(8,128)} %kernel.3, f32[1,128]{1,0:T(1,128)} %bitcast.24, f32[1,128]{1,0:T(1,128)} %bitcast.25, f32[1,128]{1,0:T(1,128)} %bitcast.26, ...), custom_call_target="tpu_custom_call" | custom-call | tf_op jit(solution)/shard_map/forward_back/pallas_call | solution.py:491
  92.3 38.2 %spread.1 = (bf16[128,64,128]{2,1,0:T(8,128)(2,1)}, f32[7,7,128]{2,1,0:T(8,128)}, f32[128,512]{1,0:T(8,128)}, f32[512,128]{1,0:T(8,128)}, f32[1,512]{1,0:T(1,128)}, /*index=5*/f32[8,128]{1,0:T(8,128)}) custom-call(bf16[128,64,128]{2,1,0:T(8,128)(2,1)} %get-tuple-element.18.cells, bf16[128,64,128]{2,1,0:T(8,128)(2,1)} %cot.3, f32[7,7,128]{2,1,0:T(8,128)} %kernel.3, ...), custom_call_target="tpu_custom_call" | custom-call | tf_op jit(solution)/shard_map/spread/pallas_call | solution.py:525
  130.5 1.4 %slice_bitcast_fusion = (f32[128]{0:T(128)}, f32[128]{0:T(128)}, f32[128]{0:T(128)}, f32[128]{0:T(128)}, f32[128]{0:T(128)}) fusion(f32[8,128]{1,0:T(8,128)} %get-tuple-element.22), kind=kLoop, calls=%fused_computation.2 | loop fusion | bytes 5120 | tf_op jit(solution)/shard_map/squeeze | solution.py:562
  131.9 0.0 copy-start.2
  131.9 0.0 copy-start.1
  131.9 0.0 copy-start.3
  131.9 0.0 copy-start
  131.9 3.1 %copy.28 = bf16[128,64,128]{2,1,0:T(8,128)(2,1)} copy(bf16[128,64,128]{2,1,0:T(8,128)(2,1)} %get-tuple-element.41) | data formatting | bytes 4194304
  135.0 0.0 copy-done.2
  135.0 0.6 copy.29
  135.6 0.0 copy-done.1
  135.6 0.7 copy.30
  136.4 0.0 copy-done.3
  136.4 0.6 copy.31
  136.9 0.0 copy-done
  136.9 0.7 copy.32
Async XLA Ops:
  131.9 3.2 %copy-start.2 = (f32[7,7,128]{2,1,0:T(8,128)S(1)}, f32[7,7,128]{2,1,0:T(8,128)}, u32[]{:S(2)}) copy-start(f32[7,7,128]{2,1,0:T(8,128)} %get-tuple-element.42) | copy-start | bytes 75268
  131.9 3.8 %copy-start.1 = (f32[128,512]{1,0:T(8,128)S(1)}, f32[128,512]{1,0:T(8,128)}, u32[]{:S(2)}) copy-start(f32[128,512]{1,0:T(8,128)} %get-tuple-element.46) | copy-start | bytes 786436
  131.9 4.5 %copy-start.3 = (f32[1,512]{1,0:T(1,128)S(1)}, f32[1,512]{1,0:T(1,128)}, u32[]{:S(2)}) copy-start(f32[1,512]{1,0:T(1,128)} %get-tuple-element.24) | copy-start | bytes 6148
  131.9 5.1 %copy-start = (f32[512,128]{1,0:T(8,128)S(1)}, f32[512,128]{1,0:T(8,128)}, u32[]{:S(2)}) copy-start(f32[512,128]{1,0:T(8,128)} %get-tuple-element.48) | copy-start | bytes 786436

commit v3 on v2

--- a/solution.py
+++ b/solution.py
@@ -214,6 +214,7 @@
     g_dn,
     g_bup,
     g_small,
+    ahead,
     conv_w,
     edge_out,
     edge_in,
@@ -239,9 +240,15 @@
     g_bup[...] = jnp.zeros_like(g_bup)
     g_small[...] = jnp.zeros_like(g_small)
 
+    chunks = rows // (2 * count)
+    ahead[0] = conv_pairs(shifted, conv_w, 0, count)
+
     def chunk(i, carry):
         first = i * count
-        pair_out = conv_pairs(shifted, conv_w, first, count)
+        slot = lax.rem(i, 2)
+        pair_out = ahead[slot]
+        later = lax.rem(i + 1, chunks)
+        ahead[1 - slot] = conv_pairs(shifted, conv_w, later * count, count)
         conv = jnp.concatenate([pair_out[:, :chans], pair_out[:, chans:]], 0) + kbias[...]
         cot_rows = [cot[2 * (first + k) + p] for p in range(2) for k in range(count)]
         cotan = jnp.concatenate(cot_rows, 0)
@@ -250,8 +257,10 @@
         normed = centred * inv_std
         normal_out = (normed * gain[...] + shift[...]).astype(BF16)
         hidden = dot(normal_out, w_up[...]) + b_up[...]
-        bell = jnp.exp(hidden * hidden * -0.5)
-        place = 1.0 / (1.0 + jnp.abs(hidden) * (0.3275911 * 0.7071067811865476))
+        bell = jnp.exp2(hidden * hidden * (-0.5 * 1.4426950408889634))
+        under = 1.0 + jnp.abs(hidden) * (0.3275911 * 0.7071067811865476)
+        rough = pl.reciprocal(under, approx=True)
+        place = rough * (2.0 - under * rough)
         tail = place * (
             0.127414796
             + place * (-0.142248368 + place * (0.7107068705 + place * (-0.7265760135 + place * 0.5307027145)))
@@ -285,7 +294,7 @@
                 d_conv[2 * (first + k) + p] = part[k * cols : (k + 1) * cols]
         return carry
 
-    lax.fori_loop(0, rows // (2 * count), chunk, 0)
+    lax.fori_loop(0, chunks, chunk, 0)
 
     eye = (
         lax.broadcasted_iota(jnp.int32, (chans, chans), 0)
@@ -377,7 +386,7 @@
         return carry
 
     chunks = rows // (2 * count)
-    lax.fori_loop(0, chunks // 4, chunk, 0)
+    lax.fori_loop(0, chunks // 8, chunk, 0)
 
     for copy in scatter_y:
         copy.wait()
@@ -391,7 +400,7 @@
     ]
     for copy in scatter_x:
         copy.start()
-    lax.fori_loop(chunks // 4, chunks // 2, chunk, 0)
+    lax.fori_loop(chunks // 8, 3 * chunks // 8, chunk, 0)
 
     for copy in scatter_x:
         copy.wait()
@@ -406,7 +415,7 @@
     ]
     for copy in gather_x:
         copy.start()
-    lax.fori_loop(chunks // 2, 3 * chunks // 4, chunk, 0)
+    lax.fori_loop(3 * chunks // 8, 5 * chunks // 8, chunk, 0)
 
     for copy in gather_x:
         copy.wait()
@@ -417,7 +426,7 @@
     ]
     for copy in gather_y:
         copy.start()
-    lax.fori_loop(3 * chunks // 4, chunks, chunk, 0)
+    lax.fori_loop(5 * chunks // 8, chunks, chunk, 0)
     for copy in gather_y:
         copy.wait()
     at = taps * (taps + 1)
@@ -503,6 +512,7 @@
                 pltpu.VMEM((chans, units), F32),
                 pltpu.VMEM((1, units), F32),
                 pltpu.VMEM((8, chans), F32),
+                pltpu.VMEM((2, count * cols, 2 * chans), F32),
             ]
             + halo,
             compiler_params=pltpu.CompilerParams(
@@ -523,7 +533,7 @@
     factor = 1.0 / math.sqrt(rows * cols * nx * ny)
     with jax.named_scope("spread"):
         d_features, d_kern, d_wup, d_wdown, d_bup, small = pl.pallas_call(
-            functools.partial(spread_kernel, taps, count, nx, ny, factor),
+            functools.partial(spread_kernel, taps, 2 * count, nx, ny, factor),
             out_shape=[
                 shapes((rows, cols, chans), BF16),
                 shapes((taps, taps, chans), F32),

time: 138 us -> 119 us (0.86)
  Pallas kernels: 126 us -> 106 us
    pallas_call x1, Pallas kernels: 87.5 us -> 69.8 us  [local(): pl.pallas_call(functools.partial(forward_back, taps, count, nx, ny), out_...]
    pallas_call x1, Pallas kernels: 38.2 us -> 36 us  [local(): pl.pallas_call(functools.partial(spread_kernel, taps, 2 * count, nx, ny,...]
where the time goes in v3:
time: 119 us; the launch traced here: 118 us
  Pallas kernels  106 us (89%)
  local copies, waits for them, and re-layouts  9.81 us (8%)
  other arithmetic  1.4 us (1%)
    pallas_call x1, Pallas kernels, local(): pl.pallas_call(functools.partial(forward_back, taps, count, nx, ny), out_...  69.8 us
    pallas_call x1, Pallas kernels, local(): pl.pallas_call(functools.partial(spread_kernel, taps, 2 * count, nx, ny,...  36 us
    unnamed x15, local copies, waits for them, and re-layouts  8.42 us

profile of v3, /device:TPU:0, one launch (start us, length us, event | category | flops | bytes accessed | tf_op | source)
XLA Modules:
  0.0 117.8 jit_solution(14581139137239673097)
XLA Ops:
  0.6 1.7 %copy.21 = bf16[128,512]{0,1:T(8,128)(2,1)} copy(bf16[128,512]{1,0:T(8,128)(2,1)} %w_up.1) | data formatting | bytes 262144 | tf_op args[6]
  2.3 1.0 copy.22
  3.3 1.4 %fusion.w_dn_t = bf16[128,512]{1,0:T(8,128)(2,1)} fusion(bf16[512,128]{0,1:T(8,128)(2,1)S(1)} %copy.22, f32[128]{0:T(128)} %param.21), kind=kLoop, calls=%fused_computation.1 | loop fusion | flops 196608 | bytes 262656 | tf_op jit(solution)/shard_map/convert_element_type | solution.py:495
  4.7 69.8 %forward_back.1 = (bf16[128,64,128]{2,1,0:T(8,128)(2,1)}, f32[1280,128]{1,0:T(8,128)}) custom-call(bf16[128,64,128]{2,1,0:T(8,128)(2,1)} %cells.1, bf16[128,64,128]{2,1,0:T(8,128)(2,1)} %cot.3, f32[7,7,128]{2,1,0:T(8,128)} %kernel.3, f32[1,128]{1,0:T(1,128)} %bitcast.24, f32[1,128]{1,0:T(1,128)} %bitcast.25, f32[1,128]{1,0:T(1,128)} %bitcast.26, ...), custom_call_target="tpu_custom_call" | custom-call | tf_op jit(solution)/shard_map/forward_back/pallas_call | solution.py:500
  74.6 36.0 %spread.1 = (bf16[128,64,128]{2,1,0:T(8,128)(2,1)}, f32[7,7,128]{2,1,0:T(8,128)}, f32[128,512]{1,0:T(8,128)}, f32[512,128]{1,0:T(8,128)}, f32[1,512]{1,0:T(1,128)}, /*index=5*/f32[8,128]{1,0:T(8,128)}) custom-call(bf16[128,64,128]{2,1,0:T(8,128)(2,1)} %get-tuple-element.18.cells, bf16[128,64,128]{2,1,0:T(8,128)(2,1)} %cot.3, f32[7,7,128]{2,1,0:T(8,128)} %kernel.3, ...), custom_call_target="tpu_custom_call" | custom-call | tf_op jit(solution)/shard_map/spread/pallas_call | solution.py:535
  110.6 1.4 %slice_bitcast_fusion = (f32[128]{0:T(128)}, f32[128]{0:T(128)}, f32[128]{0:T(128)}, f32[128]{0:T(128)}, f32[128]{0:T(128)}) fusion(f32[8,128]{1,0:T(8,128)} %get-tuple-element.22), kind=kLoop, calls=%fused_computation.2 | loop fusion | bytes 5120 | tf_op jit(solution)/shard_map/squeeze | solution.py:572
  112.0 0.0 copy-start.2
  112.0 0.0 copy-start.1
  112.0 0.0 copy-start.3
  112.0 0.0 copy-start
  112.0 3.1 %copy.28 = bf16[128,64,128]{2,1,0:T(8,128)(2,1)} copy(bf16[128,64,128]{2,1,0:T(8,128)(2,1)} %get-tuple-element.41) | data formatting | bytes 4194304
  115.2 0.0 copy-done.2
  115.2 0.6 copy.29
  115.8 0.0 copy-done.1
  115.8 0.7 copy.30
  116.5 0.0 copy-done.3
  116.5 0.6 copy.31
  117.1 0.0 copy-done
  117.1 0.7 copy.32
Async XLA Ops:
  112.0 3.2 %copy-start.2 = (f32[7,7,128]{2,1,0:T(8,128)S(1)}, f32[7,7,128]{2,1,0:T(8,128)}, u32[]{:S(2)}) copy-start(f32[7,7,128]{2,1,0:T(8,128)} %get-tuple-element.42) | copy-start | bytes 75268
  112.0 3.8 %copy-start.1 = (f32[128,512]{1,0:T(8,128)S(1)}, f32[128,512]{1,0:T(8,128)}, u32[]{:S(2)}) copy-start(f32[128,512]{1,0:T(8,128)} %get-tuple-element.46) | copy-start | bytes 786436
  112.0 4.5 %copy-start.3 = (f32[1,512]{1,0:T(1,128)S(1)}, f32[1,512]{1,0:T(1,128)}, u32[]{:S(2)}) copy-start(f32[1,512]{1,0:T(1,128)} %get-tuple-element.24) | copy-start | bytes 6148
  112.0 5.1 %copy-start = (f32[512,128]{1,0:T(8,128)S(1)}, f32[512,128]{1,0:T(8,128)}, u32[]{:S(2)}) copy-start(f32[512,128]{1,0:T(8,128)} %get-tuple-element.48) | copy-start | bytes 786436
